TPU v7x, 256 devices: a whole 4x4x8 slice. The times are simulated.
256 devices in a mesh: dp: 4 (over z_lo), fsdp: 64 (over z_hi, y, x, core).
Axes of the slice: x: 4, y: 4, z: 8 (z_hi: 2, z_lo: 4; z = z_hi * 4 + z_lo), core: 2. Of those that a mesh axis runs over, the one named last changes fastest.
Arguments:
- grads: bfloat16 [4, 256, 2048, 256], P('dp', None, 'fsdp'), may hold values from -6 to 6
- owner: int32 [256], replicated, may hold values from 0 to 63, as said below
Outputs:
- owned: bfloat16 [4, 64, 2, 2048, 256], P('dp', 'fsdp')
Inputs may be any that keep to these rules, and one draw needn't show every extreme that they name: In each block of 64 consecutive matrices no owner appears more than 2 times, and some owner appears exactly 2 times.
All inputs are finite; a program needn't handle non-finite values.
Results may differ from a plain program's by a relative error of at most 0.02.
Values may be sent and summed in bfloat16 or wider, within the bound.
A program may use at most 64 MiB of HBM per device.

v0:
```python
import math

import jax
import jax.numpy as jnp
from jax import lax
from jax.sharding import PartitionSpec as P

CAP = 2
ITERS = 3


def newton(matrix, scale_out):
    values = matrix.astype(jnp.float32)
    norm = jnp.sqrt(jnp.sum(values * values))
    state = (values / (norm + 1e-07)).astype(jnp.bfloat16)
    for step in range(ITERS):
        gram = lax.dot_general(
            state, state, (((0,), (0,)), ((), ())), preferred_element_type=jnp.float32
        ).astype(jnp.bfloat16)
        square = jnp.dot(gram, gram, preferred_element_type=jnp.float32)
        poly = (-4.775 * gram.astype(jnp.float32) + 2.0315 * square).astype(jnp.bfloat16)
        update = 3.4445 * state.astype(jnp.float32) + jnp.dot(
            state, poly, preferred_element_type=jnp.float32
        )
        if step + 1 < ITERS:
            state = update.astype(jnp.bfloat16)
        else:
            state = (update * scale_out).astype(jnp.bfloat16)
    return state


def dispatch(shards, target, tier, tiers, devices):
    device_ids = jnp.arange(devices, dtype=jnp.int32)
    tier_ids = jnp.arange(tiers, dtype=jnp.int32)
    select = (tier[None, None, :] == tier_ids[:, None, None]) & (
        target[None, None, :] == device_ids[None, :, None]
    )
    return jnp.einsum(
        "sdj,jrc->sdrc", select.astype(jnp.bfloat16), shards, preferred_element_type=jnp.float32
    ).astype(jnp.bfloat16)


def orthogonalize(stack, live, scale_out):
    results = []
    for position in range(stack.shape[0]):
        results.append(
            lax.cond(
                position < live,
                lambda item: newton(item, scale_out),
                jnp.zeros_like,
                stack[position],
            )
        )
    return jnp.stack(results)


def per_device(grads, owner):
    local = grads[0]
    matrices, rows_local, cols = local.shape
    groups = lax.axis_size("dp")
    devices = lax.axis_size("fsdp")
    per_block = matrices // groups
    rows = rows_local * devices
    scale_out = 0.2 * math.sqrt(max(rows, cols))
    summed = lax.psum_scatter(
        local.astype(jnp.float32).astype(jnp.bfloat16), "dp", scatter_dimension=0, tiled=True
    )
    mine = lax.axis_index("fsdp")
    block_owner = lax.dynamic_slice_in_dim(owner, lax.axis_index("dp") * per_block, per_block)
    index = jnp.arange(per_block, dtype=jnp.int32)
    earlier = (block_owner[None, :] == block_owner[:, None]) & (index[None, :] < index[:, None])
    slot = jnp.sum(earlier.astype(jnp.int32), axis=1)
    load = jnp.sum((block_owner == mine).astype(jnp.int32))
    outgoing = dispatch(summed, block_owner, slot, CAP, devices)
    gathered = lax.all_to_all(outgoing, "fsdp", split_axis=1, concat_axis=1, tiled=True).reshape(
        CAP, rows, cols
    )
    owned = orthogonalize(gathered, load, scale_out)
    return owned[None, None]


def solution(mesh):
    placed = (P("dp", None, "fsdp", None), P())
    return jax.shard_map(
        per_device,
        mesh=mesh,
        in_specs=placed,
        out_specs=P("dp", "fsdp", None, None, None),
        check_vma=False,
    )
```

profile of v0, /device:TPU:74, one launch (start us, length us, event | category | flops | bytes accessed | tf_op | source)
XLA Modules:
  0.0 192.7 jit_solution(1901486159726315932)
XLA Ops:
  6.5 0.0 reduce-scatter.2.cloned.1.call-start
  6.5 0.0 copy-start.1
  6.5 0.7 reduce-scatter.2.cloned.1.call-update
  7.3 0.0 copy-done.1
  7.3 0.7 fusion.73
  8.0 0.2 convert_reduce_fusion
  8.2 86.3 %reduce-scatter.2.cloned.1.call-done = bf16[64,32,256]{2,1,0:T(8,128)(2,1)} async-done(((bf16[256,32,256]{2,1,0:T(8,128)(2,1)}), bf16[64,32,256]{2,1,0:T(8,128)(2,1)}) %reduce-scatter.2.cloned.1.call-update) | async-done | bytes 1048592 | tf_op jit(solution)/shard_map/reduce_scatter | solution.py:65
  94.5 2.1 %convolution_convert_fusion.4 = bf16[2,64,32,256]{3,1,2,0:T(8,128)(2,1)S(1)} fusion(bf16[64,32,256]{2,1,0:T(8,128)(2,1)} %reduce-scatter.2.cloned.1.call-done, pred[64,64]{1,0:T(8,128)(4,1)S(1)} %iota_compare_fusion, pred[2,64]{1,0:T(4,128)(4,1)S(1)} %iota_compare_fusion.2), kind=kOutput, calls=%fused_computation.89 | convolution fusion | flops 135274496 | bytes 3149952 | tf_op jit(solution)/shard_map/sdj,jrc->sdrc/dot_general | solution.py:38
  96.6 2.5 %copy.10 = bf16[2,64,32,256]{3,2,0,1:T(8,128)(2,1)} copy(bf16[2,64,32,256]{3,1,2,0:T(8,128)(2,1)S(1)} %convolution_convert_fusion.4) | data formatting | bytes 4194304 | tf_op jit(solution)/shard_map/convert_element_type | solution.py:40
  99.1 10.5 %all-to-all-start = ((bf16[2,64,32,256]{3,2,0,1:T(8,128)(2,1)}), bf16[2,64,32,256]{3,2,0,1:T(8,128)(2,1)}, u32[]{:S(2)}, u32[]{:S(2)}) async-start(bf16[2,64,32,256]{3,2,0,1:T(8,128)(2,1)} %copy.10), calls=%async_computation.1 | async-start | bytes 4194304 | tf_op jit(solution)/shard_map/all_to_all | solution.py:75
  110.8 51.1 %all-to-all-done = bf16[2,64,32,256]{3,2,0,1:T(8,128)(2,1)} async-done(((bf16[2,64,32,256]{3,2,0,1:T(8,128)(2,1)}), bf16[2,64,32,256]{3,2,0,1:T(8,128)(2,1)}, u32[]{:S(2)}, u32[]{:S(2)}) %all-to-all-start) | async-done | bytes 2097184 | tf_op jit(solution)/shard_map/all_to_all | solution.py:75
  161.9 2.8 %copy.11 = bf16[2,64,32,256]{3,1,2,0:T(8,128)(2,1)S(1)} copy(bf16[2,64,32,256]{3,2,0,1:T(8,128)(2,1)} %all-to-all-done) | data formatting | bytes 4194304 | tf_op jit(solution)/shard_map/all_to_all | solution.py:75
  164.7 12.3 %conditional.3 = (bf16[1,2048,256]{2,1,0:T(8,128)(2,1)}) conditional(s32[]{:T(128)} %convert_element_type.142, () %tuple.22, bf16[2,64,32,256]{3,1,2,0:T(8,128)(2,1)S(1)} %copy.11), branch_computations={%region_6.0_spmd, %region_7.0_spmd} | conditional | flops 1722417152 | bytes 19660864 | solution.py:47
  164.7 1.1 fusion.38
  166.6 0.2 fusion.39
  166.8 0.5 fusion.46
  167.3 1.6 copy.8
  168.9 2.2 %fusion.35 = bf16[2048,256]{1,0:T(8,128)(2,1)S(1)} fusion(bf16[2048,256]{1,0:T(8,128)(2,1)} %bitcast.58, bf16[256,256]{1,0:T(8,128)(2,1)S(1)} %fusion.46), kind=kOutput, calls=%fused_computation.51 | convolution fusion | flops 304414720 | bytes 2228224 | tf_op jit(solution)/shard_map/cond/branch_1_fun/dot_general | solution.py:22
  171.1 0.5 convolution_convert_fusion.3
  171.6 1.6 fusion.36
  173.2 0.0 copy-start
  173.2 2.1 %convolution_convert_fusion.2 = bf16[256,256]{1,0:T(8,128)(2,1)S(1)} fusion(bf16[2048,256]{1,0:T(8,128)(2,1)} %fusion.36), kind=kOutput, calls=%fused_computation.67 | convolution fusion | flops 268500992 | bytes 1179648 | tf_op jit(solution)/shard_map/cond/branch_1_fun/dot_general | solution.py:17
  175.3 0.0 copy-done
  175.3 1.7 fusion.37
  177.0 6.1 %conditional.2 = (bf16[1,2048,256]{2,1,0:T(8,128)(2,1)S(1)}) conditional(s32[]{:T(128)} %convert_element_type.139, () %tuple.21, bf16[2,64,32,256]{3,1,2,0:T(8,128)(2,1)S(1)} %copy.11), branch_computations={%region_3.0_spmd, %region_4.0_spmd} | conditional | flops 1722417152 | bytes 15466532 | solution.py:47
  177.0 1.1 fusion.5
  178.8 0.2 fusion.6
  179.1 0.5 fusion.13
  179.6 0.6 copy.7
  180.2 0.6 fusion.2
  180.8 0.5 convolution_convert_fusion.1
  181.3 0.7 fusion.3
  182.0 0.5 convolution_convert_fusion
  182.4 0.7 fusion.4
  183.1 2.7 %maximum_bitcast_fusion = bf16[1,1,2,2048,256]{4,3,2,1,0:T(8,128)(2,1)} fusion(bf16[1,2048,256]{2,1,0:T(8,128)(2,1)} %get-tuple-element.22, bf16[1,2048,256]{2,1,0:T(8,128)(2,1)S(1)} %get-tuple-element.21), kind=kLoop, calls=%fused_computation.88 | loop fusion | flops 1048576 | bytes 4194304 | tf_op jit(solution)/shard_map/broadcast_in_dim | solution.py:79
  (2 shorter events, 0.0 us)
Async XLA Ops:
  6.5 88.0 %reduce-scatter.2.cloned.1.call-start = ((), (), s32[]{:S(2)}) async-start(), calls=%async_computation.2 | async-start | bytes 5242880 | tf_op jit(solution)/shard_map/reduce_scatter | solution.py:65
  6.5 0.7 copy-start.1
  99.1 62.8 %all-to-all-start = ((bf16[2,64,32,256]{3,2,0,1:T(8,128)(2,1)}), bf16[2,64,32,256]{3,2,0,1:T(8,128)(2,1)}, u32[]{:S(2)}, u32[]{:S(2)}) async-start(bf16[2,64,32,256]{3,2,0,1:T(8,128)(2,1)} %copy.10), calls=%async_computation.1 | async-start | bytes 4194304 | tf_op jit(solution)/shard_map/all_to_all | solution.py:75
  173.2 2.1 %copy-start = (bf16[2048,256]{1,0:T(8,128)(2,1)S(1)}, bf16[2048,256]{1,0:T(8,128)(2,1)}, u32[]{:S(2)}) copy-start(bf16[2048,256]{1,0:T(8,128)(2,1)} %fusion.36) | copy-start | bytes 3145732 | tf_op jit(solution)/shard_map/cond
Sparse Core Ops, SparseCore 0:
  9.9 84.5 reduce-scatter.1
where the time goes:
time: 193 us
  waiting for transfers between devices  138 us (72%)
  between operations  14.7 us (8%)
  matrix products  14.1 us (7%)
  starting transfers between devices  10.5 us (5%)
  local copies, waits for them, and re-layouts  7.43 us (4%)
  other arithmetic  6.41 us (3%)
    reduce_scatter x1, waiting for transfers between devices, per_device(): lax.psum_scatter(local.astype(jnp.float32).astype(jnp.bfloat16), 'dp', sc...  86.3 us
    all_to_all x1, waiting for transfers between devices, per_device(): lax.all_to_all(outgoing, 'fsdp', split_axis=1, concat_axis=1, tiled=True)  51.1 us
    all_to_all x1, starting transfers between devices, per_device(): lax.all_to_all(outgoing, 'fsdp', split_axis=1, concat_axis=1, tiled=True)  10.5 us
    dot_general x6, matrix products, newton(): jnp.dot(state, poly, preferred_element_type=jnp.float32)  7.48 us
    dot_general x6, matrix products, newton(): lax.dot_general(state, state, (((0,), (0,)), ((), ())), preferred_element...  4.52 us
  transfers between devices with their start and end apart: 2, of which 2 were waited for; matrix products, arithmetic and copies ran while one was open for 0% of the time, Pallas kernels for 0%

commit v1 on v0

v1 whole, which is shorter than its diff:
```python
import functools
import math

import jax
import jax.numpy as jnp
from jax import lax
from jax.experimental import pallas as pl
from jax.experimental.pallas import tpu as pltpu
from jax.sharding import PartitionSpec as P

MESH = pl.DeviceIdType.MESH
CAP = 2
HALVES = 2
PLANE = 32
CHUNKS = 4
TR, TC = 16, 128
PER = 64
SURE = 24
FULL = PER - SURE
ORIGIN = ((1, 0), (1, 1), (0, 3), (0, 2), (0, 1))
BACK = ((1, 3), (1, 2), (0, 0))
LISTS = ORIGIN + BACK


def size(flow):
    return SURE if flow in ((1, 1), (1, 2)) else FULL


def exchange(tab_ref, grads_ref, out_ref, g0, g1, g2, g3, own, a, b, c, xf, xs, sf, dsp,
             g_sem, a_s, a_r, b_s, b_r, c_s, c_r, x_s, x_r, u_s, u_r, p_s, p_r):
    gv = (g0, g1, g2, g3)
    g = lax.axis_index("dp")
    f = lax.axis_index("fsdp")
    h, me = f // PLANE, f % PLANE
    z = h * 4 + g
    side = g // 2
    dirn = 1 - 2 * side
    outer = (g == 0) | (g == 3)
    inner = jnp.logical_not(outer)

    def along_z(step):
        zz = (z + step + 16) % 8
        return (zz % 4, (zz // 4) * PLANE + me)

    def in_plane(j):
        return (g, h * PLANE + (me + j) % PLANE)

    def block_of(beta):
        return beta + side * (3 - 2 * beta)

    def load(beta):
        return pltpu.make_async_copy(
            grads_ref.at[pl.ds(block_of(beta) * PER, PER)], gv[beta], g_sem.at[beta])

    for beta in (0, 1, 3, 2):
        load(beta).start()

    barrier = pltpu.get_barrier_semaphore()
    for hop in (dirn, -dirn, -2 * dirn):
        pl.semaphore_signal(barrier, inc=1, device_id=along_z(hop), device_id_type=MESH)

    @pl.when(inner)
    def _():
        pl.semaphore_signal(barrier, inc=1, device_id=along_z(4), device_id_type=MESH)

    def greet(j, carry):
        pl.semaphore_signal(barrier, inc=1, device_id=in_plane(j), device_id_type=MESH)
        return carry

    lax.fori_loop(1, PLANE, greet, 0)

    def remote(src, dst, send, recv, hop):
        return pltpu.make_async_remote_copy(
            src_ref=src, dst_ref=dst, send_sem=send, recv_sem=recv,
            device_id=along_z(hop), device_id_type=MESH)

    def part(ref, flow, n, k):
        return ref.at[n, k, pl.ds(0, size(flow))]

    def send_a(n, k):
        flow = ORIGIN[n]
        return remote(part(own, flow, n, k), part(a, flow, n, k), a_s.at[n, k], a_r.at[n, k], dirn)

    def send_b(n, k):
        flow = ORIGIN[n]
        return remote(part(a, flow, n, k), part(b, flow, n, k), b_s.at[n, k], b_r.at[n, k], dirn)

    def send_c(n, k):
        flow = BACK[n]
        return remote(part(b, flow, n, k), part(c, flow, n, k), c_s.at[n, k], c_r.at[n, k], -dirn)

    def send_x(n, k):
        count = pl.ds(0, size(BACK[n]))
        return remote(c.at[n, k, count], xf.at[k, count], x_s.at[n, k], x_r.at[k], -(n + 1) * dirn)

    def send_u(k):
        both = pl.ds(SURE, FULL - SURE)
        return remote(sf.at[k, both], xf.at[k, both], u_s.at[k], u_r.at[k], 4)

    def gather(n):
        kind, beta = LISTS[n]
        row = block_of(beta) * HALVES + h + kind * (1 - 2 * h)
        src = gv[beta]

        def body(i, carry):
            value = src[tab_ref[row, i]]
            for k in range(CHUNKS):
                r, q = k // 2, k % 2
                own[n, k, i] = value[r * TR:(r + 1) * TR, q * TC:(q + 1) * TC]
            return carry

        lax.fori_loop(0, size(LISTS[n]), body, 0, unroll=4)

    for n in range(len(LISTS)):
        if n in (0, 1, 2, 3):
            load(LISTS[n][1]).wait()
        gather(n)
        if n == 0:
            @pl.when(outer)
            def _():
                pl.semaphore_wait(barrier, 3 + PLANE - 1)

            @pl.when(inner)
            def _():
                pl.semaphore_wait(barrier, 4 + PLANE - 1)
        if n < len(ORIGIN):
            @pl.when(outer)
            def _():
                send_a(n, 0).start()

    def add(n, dst, srcs):
        count = size(LISTS[n])
        lanes = pl.ds(0, count)

        def total(k):
            value = own[n, k, lanes].astype(jnp.float32)
            for src, m in srcs:
                value += src[m, k, lanes].astype(jnp.float32)
            return value.astype(jnp.bfloat16)

        return total

    def spread(j, k):
        p = (me + j) % PLANE
        return pltpu.make_async_remote_copy(
            src_ref=dsp.at[k, p], dst_ref=out_ref.at[:, k // 2, k % 2, me],
            send_sem=p_s.at[j], recv_sem=p_r.at[me], device_id=in_plane(j), device_id_type=MESH)

    def step(k, carry):
        @pl.when(outer)
        def _():
            @pl.when(k + 1 < CHUNKS)
            def _():
                for n in range(len(ORIGIN)):
                    send_a(n, k + 1).start()

            for n, flow in enumerate(BACK):
                send_c(n, k).wait_recv()
                total = add(5 + n, None, [(c, n)])(k)
                if n < 2:
                    c[n, k, pl.ds(0, size(flow))] = total
                    send_x(n, k).start()
                else:
                    sf[k] = total
            send_x(0, k).wait_recv()

        @pl.when(inner)
        def _():
            def forward(n):
                send_a(n, k).wait_recv()
                a[n, k, pl.ds(0, size(ORIGIN[n]))] = add(n, None, [(a, n)])(k)
                send_b(n, k).start()

            def back(n):
                send_b(n, k).wait_recv()
                b[n, k, pl.ds(0, size(BACK[n]))] = add(5 + n, None, [(b, n)])(k)
                send_c(n, k).start()

            forward(0)
            forward(1)
            back(0)
            forward(2)
            back(1)
            forward(3)
            back(2)
            send_a(4, k).wait_recv()
            send_b(3, k).wait_recv()
            sf[k] = add(4, None, [(a, 4), (b, 3)])(k)
            send_u(k).start()
            send_x(1, k).wait_recv()
            send_u(k).wait_recv()

        xs[...] = xf[k]

        def fill(j, carry):
            p = (me + j) % PLANE
            for s in range(CAP):
                i = tab_ref[8 + s, h * PLANE + p]
                dsp[k, p, s, h] = sf[k, i]
                dsp[k, p, s, 1 - h] = xs[i]
            spread(j, k).start()
            return carry

        lax.fori_loop(1, PLANE, fill, 0)
        for s in range(CAP):
            i = tab_ref[8 + s, h * PLANE + me]
            dsp[k, me, s, h] = sf[k, i]
            dsp[k, me, s, 1 - h] = xs[i]
        pltpu.make_async_copy(
            dsp.at[k, me], out_ref.at[:, k // 2, k % 2, me], p_r.at[me]).start()
        return carry

    lax.fori_loop(0, CHUNKS, step, 0)

    def finish(k, carry):
        @pl.when(outer)
        def _():
            for n in range(5):
                send_a(n, k).wait_send()
            for n in range(2):
                send_x(n, k).wait_send()

        @pl.when(inner)
        def _():
            for n in range(4):
                send_b(n, k).wait_send()
            for n in range(3):
                send_c(n, k).wait_send()
            send_u(k).wait_send()

        return carry

    lax.fori_loop(0, CHUNKS, finish, 0)

    def sent(j, carry):
        whole = dsp.at[:, (me + j) % PLANE]
        pltpu.make_async_copy(whole, whole, p_s.at[j]).wait()
        return carry

    lax.fori_loop(1, PLANE, sent, 0)

    def landed(src, carry):
        whole = out_ref.at[:, :, :, src]
        pltpu.make_async_copy(whole, whole, p_r.at[src]).wait()
        return carry

    lax.fori_loop(0, PLANE, landed, 0)


def run_exchange(tab, owner, grads):
    rows, cols = grads.shape[1:]
    dma = pltpu.SemaphoreType.DMA
    vmem = lambda *shape: pltpu.VMEM(shape, jnp.bfloat16)
    return pl.pallas_call(
        exchange,
        out_shape=jax.ShapeDtypeStruct((CAP, 2, 2, PLANE, HALVES, TR, TC), jnp.bfloat16),
        in_specs=[
            pl.BlockSpec(memory_space=pltpu.SMEM),
            pl.BlockSpec(memory_space=pl.ANY),
        ],
        out_specs=pl.BlockSpec(memory_space=pl.ANY),
        scratch_shapes=[
            *[vmem(PER, rows, cols) for _ in range(4)],
            vmem(8, CHUNKS, FULL, TR, TC),
            vmem(5, CHUNKS, FULL, TR, TC),
            vmem(4, CHUNKS, FULL, TR, TC),
            vmem(3, CHUNKS, FULL, TR, TC),
            vmem(CHUNKS, FULL, TR, TC),
            vmem(FULL, TR, TC),
            vmem(CHUNKS, FULL, TR, TC),
            vmem(CHUNKS, PLANE, CAP, HALVES, TR, TC),
            dma((4,)),
            dma((5, CHUNKS)), dma((5, CHUNKS)),
            dma((4, CHUNKS)), dma((4, CHUNKS)),
            dma((3, CHUNKS)), dma((3, CHUNKS)),
            dma((2, CHUNKS)), dma((CHUNKS,)),
            dma((CHUNKS,)), dma((CHUNKS,)),
            dma((PLANE,)), dma((PLANE,)),
        ],
        compiler_params=pltpu.CompilerParams(
            collective_id=1, has_side_effects=True, vmem_limit_bytes=48 * 2**20),
        name="exchange",
    )(tab, grads)


def run_any(tab, owner, grads):
    rows, cols = grads.shape[1:]
    parts = lax.all_to_all(grads, "dp", split_axis=0, concat_axis=0, tiled=True)
    parts = parts.reshape(-1, PER, rows, cols).astype(jnp.float32)
    summed = jnp.sum(parts, axis=0).astype(jnp.bfloat16)
    own = lax.dynamic_slice_in_dim(owner, lax.axis_index("dp") * PER, PER)
    index = jnp.arange(PER, dtype=jnp.int32)
    same = own[None, :] == own[:, None]
    slot = jnp.sum((same & (index[None, :] < index[:, None])).astype(jnp.int32), axis=1)
    hit = (slot[None, None, :] == jnp.arange(CAP)[:, None, None]) & (
        own[None, None, :] == jnp.arange(HALVES * PLANE)[None, :, None])
    sends = jnp.einsum(
        "sdj,jrc->sdrc", hit.astype(jnp.bfloat16), summed, preferred_element_type=jnp.float32
    ).astype(jnp.bfloat16)
    got = lax.all_to_all(sends, "fsdp", split_axis=1, concat_axis=1, tiled=True)
    got = got.reshape(CAP, HALVES, PLANE, 2, TR, 2, TC)
    return got.transpose(0, 3, 5, 2, 1, 4, 6)


def newton(scale_out, tab_ref, x_ref, out_ref):
    cols = 2 * TC
    half_rows = PLANE * HALVES * TR
    f32 = jnp.float32
    row = lax.broadcasted_iota(jnp.int32, (cols, cols), 0)
    col = lax.broadcasted_iota(jnp.int32, (cols, cols), 1)
    eye = (row == col).astype(f32)
    live = tab_ref[10, lax.axis_index("fsdp")]

    def dot(p, q):
        return jnp.dot(p.astype(jnp.bfloat16), q.astype(jnp.bfloat16), preferred_element_type=f32)

    def half(s, r):
        return jnp.concatenate(
            [x_ref[s, r, c].reshape(half_rows, TC) for c in range(2)], axis=1)

    grams, maps, scales = [], [], []
    for s in range(CAP):
        gram = jnp.zeros((cols, cols), f32)
        for r in range(2):
            part = half(s, r)
            gram += lax.dot_general(part, part, (((0,), (0,)), ((), ())), preferred_element_type=f32)
        norm = jnp.sqrt(jnp.sum(gram * eye, keepdims=True))
        inv = 1.0 / (norm + 1e-07)
        grams.append(gram * inv * inv)
        scales.append(inv * scale_out)
        maps.append(None)
    for it in range(3):
        for s in range(CAP):
            gram = grams[s]
            poly = 3.4445 * eye - 4.775 * gram + 2.0315 * dot(gram, gram)
            maps[s] = poly if maps[s] is None else dot(maps[s], poly)
            if it < 2:
                grams[s] = dot(poly, dot(gram, poly))
    for s in range(CAP):
        last = (maps[s] * scales[s]).astype(jnp.bfloat16)
        for r in range(2):
            y = jnp.dot(half(s, r), last, preferred_element_type=f32)
            y = jnp.where(s < live, y, 0.0).astype(jnp.bfloat16)
            y = y.reshape(PLANE, HALVES, TR, cols)
            for hh in range(HALVES):
                out_ref[s, hh, :, r] = y[:, hh]


def tables(owner_ref, tab_ref):
    f32 = jnp.float32
    g = lax.axis_index("dp")
    h = lax.axis_index("fsdp") // PLANE
    groups = owner_ref.shape[1] // PER
    owner = jnp.concatenate([owner_ref[:, b * PER:(b + 1) * PER] for b in range(groups)], axis=0)
    sub = lax.broadcasted_iota(jnp.int32, (PER, PER), 0)
    lane = lax.broadcasted_iota(jnp.int32, (PER, PER), 1)
    before = (sub < lane).astype(f32)
    index = lax.broadcasted_iota(jnp.int32, (groups, PER), 1).astype(f32)
    far = (owner >= PLANE).astype(f32)
    ones_before = jnp.dot(far, before, preferred_element_type=f32)
    near_count = PER - jnp.sum(far, axis=1, keepdims=True)
    order = jnp.where(far > 0, near_count + ones_before, index - ones_before)
    key = jnp.where(order >= FULL, order - FULL, jnp.where(order >= SURE, order, -1.0))
    subf = sub.astype(f32)
    weight = lax.broadcasted_iota(jnp.int32, (8, PER), 1).astype(f32)

    def rowdot(left, hot):
        out = lax.dot_general(left, hot, (((1,), (1,)), ((), ())), preferred_element_type=f32)
        return out[0:1].astype(jnp.int32)

    tab_ref[...] = jnp.zeros_like(tab_ref)
    for blk in range(groups):
        for half, keys in enumerate((order, key)):
            hot = (keys[blk:blk + 1] == subf).astype(f32)
            tab_ref[2 * blk + half:2 * blk + half + 1, 0:PER] = rowdot(weight, hot)
    mine = lax.broadcasted_iota(jnp.int32, (groups, PER), 0) == g
    own = jnp.sum(jnp.where(mine, owner, 0), axis=0, keepdims=True)
    place = jnp.sum(jnp.where(mine, jnp.where(h == 0, order, key), 0.0), axis=0, keepdims=True)
    has = (own == sub).astype(f32)
    slot = jnp.sum(has * jnp.dot(has, before, preferred_element_type=f32), axis=0, keepdims=True)
    place = jnp.broadcast_to(place, (8, PER))
    for s in range(CAP):
        tab_ref[8 + s:9 + s, 0:PER] = rowdot(place, has * (slot == s).astype(f32))
    tab_ref[10:11, 0:PER] = rowdot(jnp.ones((8, PER), f32), has)
    good = (near_count >= SURE) & (near_count <= FULL)
    good = jnp.min(good.astype(f32), axis=0, keepdims=True).astype(jnp.int32)
    tab_ref[11:12, 0:PER] = jnp.broadcast_to(good, (1, PER))


def per_device(grads, owner):
    local = grads[0]
    mats, rows, cols = local.shape
    scale_out = 0.2 * math.sqrt(max(rows * PLANE * HALVES, cols))
    tab = pl.pallas_call(
        tables,
        out_shape=jax.ShapeDtypeStruct((16, 128), jnp.int32),
        in_specs=[pl.BlockSpec(memory_space=pltpu.VMEM)],
        out_specs=pl.BlockSpec(memory_space=pltpu.VMEM),
        name="tables",
    )(owner.reshape(1, mats))
    gathered = lax.cond(tab[11, 0] == 1, run_exchange, run_any, tab, owner, local)
    owned = pl.pallas_call(
        functools.partial(newton, scale_out),
        out_shape=jax.ShapeDtypeStruct((CAP, HALVES, PLANE, 2, TR, cols), jnp.bfloat16),
        in_specs=[pl.BlockSpec(memory_space=pltpu.SMEM), pl.BlockSpec(memory_space=pltpu.VMEM)],
        out_specs=pl.BlockSpec(memory_space=pltpu.VMEM),
        compiler_params=pltpu.CompilerParams(vmem_limit_bytes=48 * 2**20),
        name="newton",
    )(tab, gathered)
    return owned.reshape(1, 1, CAP, HALVES * PLANE * rows, cols)


def solution(mesh):
    placed = (P("dp", None, "fsdp", None), P())
    return jax.shard_map(
        per_device,
        mesh=mesh,
        in_specs=placed,
        out_specs=P("dp", "fsdp", None, None, None),
        check_vma=False,
    )
```

time: 193 us -> 110 us (0.57)
  the two profiles are of different devices: /device:TPU:74 before, /device:TPU:33 now
where the time goes in v1:
time: 110 us
  Pallas kernels  109 us (99%)
    pallas_call x1, Pallas kernels, run_exchange(): pl.pallas_call(exchange, out_shape=jax.ShapeDtypeStruct((CAP, 2, 2, PLANE...  102 us
    pallas_call x1, Pallas kernels, per_device(): pl.pallas_call(functools.partial(newton, scale_out), out_shape=jax.ShapeD...  5.25 us

profile of v1, /device:TPU:33, one launch (start us, length us, event | category | flops | bytes accessed | tf_op | source)
XLA Modules:
  0.0 110.0 jit_solution(4887939808223257727)
XLA Ops:
  0.0 1.2 %tables.1.tab_ref = s32[16,128]{1,0:T(8,128)S(1)} custom-call(s32[1,256]{1,0:T(1,128)} %bitcast.21), custom_call_target="tpu_custom_call" | custom-call | tf_op jit(solution)/shard_map/tables/pallas_call | solution.py:394
  1.2 0.5 slice.4
  2.4 102.3 %conditional.1 = (bf16[2,2,2,32,2,16,128]{6,5,4,3,2,1,0:T(8,128)(2,1)S(1)}) conditional(s32[]{:T(128)} %bitcast.6, (s32[256]{0:T(256)}, bf16[256,32,256]{2,1,0:T(8,128)(2,1)}) %tuple.17, (s32[16,128]{1,0:T(8,128)S(1)}, bf16[256,32,256]{2,1,0:T(8,128)(2,1)}) %tuple.18), branch_computations={%region_0.0_spmd, %region_3.0_spmd} | conditional | flops 136872000 | bytes 37762968 | solution.py:401
  2.4 102.3 %exchange.1 = bf16[2,2,2,32,2,16,128]{6,5,4,3,2,1,0:T(8,128)(2,1)S(1)} custom-call(s32[16,128]{1,0:T(8,128)S(1)} %get-tuple-element.18.tab_ref, bf16[256,32,256]{2,1,0:T(8,128)(2,1)} %get-tuple-element.19.grads_ref), custom_call_target="tpu_custom_call" | custom-call | tf_op jit(solution)/shard_map/cond/branch_1_fun/exchange/pallas_call | solution.py:254
  104.7 5.3 %newton.1 = bf16[2,2,32,2,16,256]{5,4,3,2,1,0:T(8,128)(2,1)} custom-call(s32[16,128]{1,0:T(8,128)S(1)} %tables.1.tab_ref, bf16[2,2,2,32,2,16,128]{6,5,4,3,2,1,0:T(8,128)(2,1)S(1)} %get-tuple-element.20.x_ref), custom_call_target="tpu_custom_call" | custom-call | tf_op jit(solution)/shard_map/newton/pallas_call | solution.py:402

commit v2 on v1

--- a/solution.py
+++ b/solution.py
@@ -15,19 +15,26 @@
 CHUNKS = 4
 TR, TC = 16, 128
 PER = 64
-SURE = 24
-FULL = PER - SURE
+SURES = (28, 25, 20)
 ORIGIN = ((1, 0), (1, 1), (0, 3), (0, 2), (0, 1))
-BACK = ((1, 3), (1, 2), (0, 0))
-LISTS = ORIGIN + BACK
-
-
-def size(flow):
-    return SURE if flow in ((1, 1), (1, 2)) else FULL
-
-
-def exchange(tab_ref, grads_ref, out_ref, g0, g1, g2, g3, own, a, b, c, xf, xs, sf, dsp,
+LISTS = ORIGIN + ((1, 3), (1, 2), (0, 0))
+GATHER = ((1, (0,)), (0, (1, 2)), (3, ()), (4, (3, 4)), (2, (5, 6, 7)), (5, ()), (6, ()), (7, ()))
+ONWARD = (0, 1, 2, 3, 5, 6, 7)
+HOME = (0, 1, 2, 5, 6)
+FAR = (0, 1, 2)
+
+
+def layout(sure):
+    full = PER - sure
+    half = full // 2
+    return ((1, 0, sure), (0, 0, half), (0, half, full), (3, sure, full), (4, sure, full),
+            (2, 0, half), (2, half, full), (3, 0, sure), (4, 0, sure))
+
+
+def exchange(sure, tab_ref, grads_ref, out_ref, g0, g1, g2, g3, own, a, b, c, xf, xs, sf, dsp,
              g_sem, a_s, a_r, b_s, b_r, c_s, c_r, x_s, x_r, u_s, u_r, p_s, p_r):
+    pieces_of = layout(sure)
+    full = PER - sure
     gv = (g0, g1, g2, g3)
     g = lax.axis_index("dp")
     f = lax.axis_index("fsdp")
@@ -52,7 +59,7 @@
         return pltpu.make_async_copy(
             grads_ref.at[pl.ds(block_of(beta) * PER, PER)], gv[beta], g_sem.at[beta])
 
-    for beta in (0, 1, 3, 2):
+    for beta in (1, 0, 2, 3):
         load(beta).start()
 
     barrier = pltpu.get_barrier_semaphore()
@@ -74,27 +81,26 @@
             src_ref=src, dst_ref=dst, send_sem=send, recv_sem=recv,
             device_id=along_z(hop), device_id_type=MESH)
 
-    def part(ref, flow, n, k):
-        return ref.at[n, k, pl.ds(0, size(flow))]
-
-    def send_a(n, k):
-        flow = ORIGIN[n]
-        return remote(part(own, flow, n, k), part(a, flow, n, k), a_s.at[n, k], a_r.at[n, k], dirn)
-
-    def send_b(n, k):
-        flow = ORIGIN[n]
-        return remote(part(a, flow, n, k), part(b, flow, n, k), b_s.at[n, k], b_r.at[n, k], dirn)
-
-    def send_c(n, k):
-        flow = BACK[n]
-        return remote(part(b, flow, n, k), part(c, flow, n, k), c_s.at[n, k], c_r.at[n, k], -dirn)
-
-    def send_x(n, k):
-        count = pl.ds(0, size(BACK[n]))
-        return remote(c.at[n, k, count], xf.at[k, count], x_s.at[n, k], x_r.at[k], -(n + 1) * dirn)
+    def part(ref, m, k):
+        n, low, high = pieces_of[m]
+        return ref.at[n, k, pl.ds(low, high - low)]
+
+    def send_a(m, k):
+        return remote(part(own, m, k), part(a, m, k), a_s.at[m, k], a_r.at[m, k], dirn)
+
+    def send_b(m, k):
+        return remote(part(a, m, k), part(b, m, k), b_s.at[m, k], b_r.at[m, k], dirn)
+
+    def send_c(m, k):
+        return remote(part(b, m, k), part(c, m, k), c_s.at[m, k], c_r.at[m, k], -dirn)
+
+    def send_x(m, k):
+        n, low, high = pieces_of[m]
+        lanes = pl.ds(low, high - low)
+        return remote(c.at[n, k, lanes], xf.at[k, lanes], x_s.at[m, k], x_r.at[m, k], (-1 - n) * dirn)
 
     def send_u(k):
-        both = pl.ds(SURE, FULL - SURE)
+        both = pl.ds(sure, full - sure)
         return remote(sf.at[k, both], xf.at[k, both], u_s.at[k], u_r.at[k], 4)
 
     def gather(n):
@@ -109,13 +115,21 @@
                 own[n, k, i] = value[r * TR:(r + 1) * TR, q * TC:(q + 1) * TC]
             return carry
 
-        lax.fori_loop(0, size(LISTS[n]), body, 0, unroll=4)
-
-    for n in range(len(LISTS)):
-        if n in (0, 1, 2, 3):
+        count = sure if LISTS[n] in ((1, 1), (1, 2)) else full
+        lax.fori_loop(0, count, body, 0, unroll=4)
+
+    def start_a(n, k):
+        @pl.when(outer)
+        def _():
+            send_a(n, k).start()
+
+    loaded = []
+    for turn, (n, pieces) in enumerate(GATHER):
+        if LISTS[n][1] not in loaded:
             load(LISTS[n][1]).wait()
+            loaded.append(LISTS[n][1])
         gather(n)
-        if n == 0:
+        if turn == 0:
             @pl.when(outer)
             def _():
                 pl.semaphore_wait(barrier, 3 + PLANE - 1)
@@ -123,109 +137,140 @@
             @pl.when(inner)
             def _():
                 pl.semaphore_wait(barrier, 4 + PLANE - 1)
-        if n < len(ORIGIN):
-            @pl.when(outer)
-            def _():
-                send_a(n, 0).start()
-
-    def add(n, dst, srcs):
-        count = size(LISTS[n])
-        lanes = pl.ds(0, count)
-
-        def total(k):
-            value = own[n, k, lanes].astype(jnp.float32)
-            for src, m in srcs:
-                value += src[m, k, lanes].astype(jnp.float32)
-            return value.astype(jnp.bfloat16)
-
-        return total
-
-    def spread(j, k):
+        for m in pieces:
+            start_a(m, 0)
+
+    def total(mine, m, k, *srcs):
+        _, low, high = pieces_of[m]
+        lanes = pl.ds(low, high - low)
+        value = own[mine, k, lanes].astype(jnp.float32)
+        for src, n in srcs:
+            value += src[n, k, lanes].astype(jnp.float32)
+        return value.astype(jnp.bfloat16)
+
+    def spread(j, k, kind):
         p = (me + j) % PLANE
         return pltpu.make_async_remote_copy(
-            src_ref=dsp.at[k, p], dst_ref=out_ref.at[:, k // 2, k % 2, me],
+            src_ref=dsp.at[k, kind, p],
+            dst_ref=out_ref.at[:, k // 2, k % 2, me, h + kind * (1 - 2 * h)],
             send_sem=p_s.at[j], recv_sem=p_r.at[me], device_id=in_plane(j), device_id_type=MESH)
 
-    def step(k, carry):
+    def dispatch(k, kind):
+        def fill(p):
+            for s in range(CAP):
+                i = tab_ref[8 + s, h * PLANE + p]
+                dsp[k, kind, p, s] = xs[i] if kind else sf[k, i]
+
+        def body(j, carry):
+            fill((me + j) % PLANE)
+            spread(j, k, kind).start()
+            return carry
+
+        lax.fori_loop(1, PLANE, body, 0)
+        fill(me)
+        pltpu.make_async_copy(
+            dsp.at[k, kind, me], out_ref.at[:, k // 2, k % 2, me, h + kind * (1 - 2 * h)],
+            p_r.at[me]).start()
+
+    def step(t, carry):
+        k = t - 1
+
+        def ahead(*runs):
+            @pl.when(t < CHUNKS)
+            def _():
+                for run, *args in runs:
+                    run(*args)
+
+        def behind(*runs):
+            @pl.when(t >= 1)
+            def _():
+                for run, *args in runs:
+                    run(*args)
+
+        def from_far(*pieces):
+            for m in pieces:
+                send_x(m, k).wait_recv()
+            xs[...] = xf[k]
+            dispatch(k, 1)
+
         @pl.when(outer)
         def _():
-            @pl.when(k + 1 < CHUNKS)
-            def _():
-                for n in range(len(ORIGIN)):
-                    send_a(n, k + 1).start()
-
-            for n, flow in enumerate(BACK):
-                send_c(n, k).wait_recv()
-                total = add(5 + n, None, [(c, n)])(k)
-                if n < 2:
-                    c[n, k, pl.ds(0, size(flow))] = total
-                    send_x(n, k).start()
-                else:
-                    sf[k] = total
-            send_x(0, k).wait_recv()
+            @pl.when(t + 1 < CHUNKS)
+            def _():
+                for m in range(8):
+                    send_a(m, t + 1).start()
+
+            @pl.when(t < CHUNKS)
+            def _():
+                send_a(8, t).start()
+
+            def back(m):
+                send_c(m, t).wait_recv()
+                n, low, high = pieces_of[m]
+                c[n, t, pl.ds(low, high - low)] = total(5 + n, m, t, (c, n))
+                send_x(m, t).start()
+
+            def last(m):
+                send_c(m, k).wait_recv()
+                _, low, high = pieces_of[m]
+                sf[k, pl.ds(low, high - low)] = total(7, m, k, (c, 2))
+
+            behind((from_far, 1, 2), (last, 5), (last, 6), (dispatch, k, 0))
+            ahead((back, 0), (back, 1), (back, 2))
 
         @pl.when(inner)
         def _():
-            def forward(n):
-                send_a(n, k).wait_recv()
-                a[n, k, pl.ds(0, size(ORIGIN[n]))] = add(n, None, [(a, n)])(k)
-                send_b(n, k).start()
-
-            def back(n):
-                send_b(n, k).wait_recv()
-                b[n, k, pl.ds(0, size(BACK[n]))] = add(5 + n, None, [(b, n)])(k)
-                send_c(n, k).start()
-
-            forward(0)
-            forward(1)
-            back(0)
-            forward(2)
-            back(1)
-            forward(3)
-            back(2)
-            send_a(4, k).wait_recv()
-            send_b(3, k).wait_recv()
-            sf[k] = add(4, None, [(a, 4), (b, 3)])(k)
-            send_u(k).start()
-            send_x(1, k).wait_recv()
-            send_u(k).wait_recv()
-
-        xs[...] = xf[k]
-
-        def fill(j, carry):
-            p = (me + j) % PLANE
-            for s in range(CAP):
-                i = tab_ref[8 + s, h * PLANE + p]
-                dsp[k, p, s, h] = sf[k, i]
-                dsp[k, p, s, 1 - h] = xs[i]
-            spread(j, k).start()
-            return carry
-
-        lax.fori_loop(1, PLANE, fill, 0)
-        for s in range(CAP):
-            i = tab_ref[8 + s, h * PLANE + me]
-            dsp[k, me, s, h] = sf[k, i]
-            dsp[k, me, s, 1 - h] = xs[i]
-        pltpu.make_async_copy(
-            dsp.at[k, me], out_ref.at[:, k // 2, k % 2, me], p_r.at[me]).start()
+            def forward(m):
+                send_a(m, t).wait_recv()
+                n, low, high = pieces_of[m]
+                a[n, t, pl.ds(low, high - low)] = total(n, m, t, (a, n))
+                send_b(m, t).start()
+
+            def back(m):
+                send_b(m, t).wait_recv()
+                n, low, high = pieces_of[m]
+                b[n, t, pl.ds(low, high - low)] = total(5 + n, m, t, (b, n))
+                send_c(m, t).start()
+
+            def last(m, across, q):
+                send_a(m, q).wait_recv()
+                send_b(across, q).wait_recv()
+                _, low, high = pieces_of[m]
+                sf[q, pl.ds(low, high - low)] = total(4, m, q, (a, 4), (b, 3))
+
+            def both():
+                last(4, 3, t)
+                send_u(t).start()
+
+            def arrive():
+                send_u(k).wait_recv()
+                from_far(0)
+
+            behind((arrive,))
+            ahead((forward, 0), (forward, 1), (forward, 2), (back, 0), (forward, 3), (back, 1),
+                  (back, 2), (forward, 5), (both,), (forward, 6), (forward, 7), (back, 5))
+            behind((last, 8, 7, k))
+            ahead((back, 6))
+            behind((dispatch, k, 0))
+
         return carry
 
-    lax.fori_loop(0, CHUNKS, step, 0)
+    lax.fori_loop(0, CHUNKS + 1, step, 0)
 
     def finish(k, carry):
         @pl.when(outer)
         def _():
-            for n in range(5):
-                send_a(n, k).wait_send()
-            for n in range(2):
-                send_x(n, k).wait_send()
+            for m in range(9):
+                send_a(m, k).wait_send()
+            for m in FAR:
+                send_x(m, k).wait_send()
 
         @pl.when(inner)
         def _():
-            for n in range(4):
-                send_b(n, k).wait_send()
-            for n in range(3):
-                send_c(n, k).wait_send()
+            for m in ONWARD:
+                send_b(m, k).wait_send()
+            for m in HOME:
+                send_c(m, k).wait_send()
             send_u(k).wait_send()
 
         return carry
@@ -233,7 +278,7 @@
     lax.fori_loop(0, CHUNKS, finish, 0)
 
     def sent(j, carry):
-        whole = dsp.at[:, (me + j) % PLANE]
+        whole = dsp.at[:, :, (me + j) % PLANE]
         pltpu.make_async_copy(whole, whole, p_s.at[j]).wait()
         return carry
 
@@ -247,12 +292,13 @@
     lax.fori_loop(0, PLANE, landed, 0)
 
 
-def run_exchange(tab, owner, grads):
+def run_exchange(ident, sure, tab, owner, grads):
+    full = PER - sure
     rows, cols = grads.shape[1:]
     dma = pltpu.SemaphoreType.DMA
     vmem = lambda *shape: pltpu.VMEM(shape, jnp.bfloat16)
     return pl.pallas_call(
-        exchange,
+        functools.partial(exchange, sure),
         out_shape=jax.ShapeDtypeStruct((CAP, 2, 2, PLANE, HALVES, TR, TC), jnp.bfloat16),
         in_specs=[
             pl.BlockSpec(memory_space=pltpu.SMEM),
@@ -261,25 +307,25 @@
         out_specs=pl.BlockSpec(memory_space=pl.ANY),
         scratch_shapes=[
             *[vmem(PER, rows, cols) for _ in range(4)],
-            vmem(8, CHUNKS, FULL, TR, TC),
-            vmem(5, CHUNKS, FULL, TR, TC),
-            vmem(4, CHUNKS, FULL, TR, TC),
-            vmem(3, CHUNKS, FULL, TR, TC),
-            vmem(CHUNKS, FULL, TR, TC),
-            vmem(FULL, TR, TC),
-            vmem(CHUNKS, FULL, TR, TC),
-            vmem(CHUNKS, PLANE, CAP, HALVES, TR, TC),
+            vmem(8, CHUNKS, full, TR, TC),
+            vmem(5, CHUNKS, full, TR, TC),
+            vmem(4, CHUNKS, full, TR, TC),
+            vmem(3, CHUNKS, full, TR, TC),
+            vmem(CHUNKS, full, TR, TC),
+            vmem(full, TR, TC),
+            vmem(CHUNKS, full, TR, TC),
+            vmem(CHUNKS, HALVES, PLANE, CAP, TR, TC),
             dma((4,)),
-            dma((5, CHUNKS)), dma((5, CHUNKS)),
-            dma((4, CHUNKS)), dma((4, CHUNKS)),
+            dma((9, CHUNKS)), dma((9, CHUNKS)),
+            dma((9, CHUNKS)), dma((9, CHUNKS)),
+            dma((9, CHUNKS)), dma((9, CHUNKS)),
             dma((3, CHUNKS)), dma((3, CHUNKS)),
-            dma((2, CHUNKS)), dma((CHUNKS,)),
             dma((CHUNKS,)), dma((CHUNKS,)),
             dma((PLANE,)), dma((PLANE,)),
         ],
         compiler_params=pltpu.CompilerParams(
-            collective_id=1, has_side_effects=True, vmem_limit_bytes=48 * 2**20),
-        name="exchange",
+            collective_id=ident, has_side_effects=True, vmem_limit_bytes=48 * 2**20),
+        name=f"exchange{sure}",
     )(tab, grads)
 
 
@@ -302,7 +348,7 @@
     return got.transpose(0, 3, 5, 2, 1, 4, 6)
 
 
-def newton(scale_out, tab_ref, x_ref, out_ref):
+def newton(scale_out, tab_ref, x_ref, out_ref, y_ref, sems):
     cols = 2 * TC
     half_rows = PLANE * HALVES * TR
     f32 = jnp.float32
@@ -343,7 +389,11 @@
             y = jnp.where(s < live, y, 0.0).astype(jnp.bfloat16)
             y = y.reshape(PLANE, HALVES, TR, cols)
             for hh in range(HALVES):
-                out_ref[s, hh, :, r] = y[:, hh]
+                y_ref[s, r, hh] = y[:, hh]
+            pltpu.make_async_copy(y_ref.at[s, r], out_ref.at[s, :, :, r], sems.at[s, r]).start()
+    for s in range(CAP):
+        for r in range(2):
+            pltpu.make_async_copy(y_ref.at[s, r], out_ref.at[s, :, :, r], sems.at[s, r]).wait()
 
 
 def tables(owner_ref, tab_ref):
@@ -360,7 +410,12 @@
     ones_before = jnp.dot(far, before, preferred_element_type=f32)
     near_count = PER - jnp.sum(far, axis=1, keepdims=True)
     order = jnp.where(far > 0, near_count + ones_before, index - ones_before)
-    key = jnp.where(order >= FULL, order - FULL, jnp.where(order >= SURE, order, -1.0))
+    fewest = jnp.min(jnp.minimum(near_count, PER - near_count), axis=0, keepdims=True)
+    sure, tier = jnp.full((1, 1), float(SURES[-1]), f32), jnp.full((1, 1), float(len(SURES)), f32)
+    for number, count in reversed(tuple(enumerate(SURES))):
+        sure = jnp.where(fewest >= count, float(count), sure)
+        tier = jnp.where(fewest >= count, float(number), tier)
+    key = jnp.where(order >= PER - sure, order - (PER - sure), jnp.where(order >= sure, order, -1.0))
     subf = sub.astype(f32)
     weight = lax.broadcasted_iota(jnp.int32, (8, PER), 1).astype(f32)
 
@@ -382,9 +437,7 @@
     for s in range(CAP):
         tab_ref[8 + s:9 + s, 0:PER] = rowdot(place, has * (slot == s).astype(f32))
     tab_ref[10:11, 0:PER] = rowdot(jnp.ones((8, PER), f32), has)
-    good = (near_count >= SURE) & (near_count <= FULL)
-    good = jnp.min(good.astype(f32), axis=0, keepdims=True).astype(jnp.int32)
-    tab_ref[11:12, 0:PER] = jnp.broadcast_to(good, (1, PER))
+    tab_ref[11:12, 0:PER] = jnp.broadcast_to(tier.astype(jnp.int32), (1, PER))
 
 
 def per_device(grads, owner):
@@ -398,12 +451,17 @@
         out_specs=pl.BlockSpec(memory_space=pltpu.VMEM),
         name="tables",
     )(owner.reshape(1, mats))
-    gathered = lax.cond(tab[11, 0] == 1, run_exchange, run_any, tab, owner, local)
+    ways = [functools.partial(run_exchange, 1 + n, sure) for n, sure in enumerate(SURES)]
+    gathered = lax.switch(tab[11, 0], ways + [run_any], tab, owner, local)
     owned = pl.pallas_call(
         functools.partial(newton, scale_out),
         out_shape=jax.ShapeDtypeStruct((CAP, HALVES, PLANE, 2, TR, cols), jnp.bfloat16),
         in_specs=[pl.BlockSpec(memory_space=pltpu.SMEM), pl.BlockSpec(memory_space=pltpu.VMEM)],
-        out_specs=pl.BlockSpec(memory_space=pltpu.VMEM),
+        out_specs=pl.BlockSpec(memory_space=pl.ANY),
+        scratch_shapes=[
+            pltpu.VMEM((CAP, 2, HALVES, PLANE, TR, cols), jnp.bfloat16),
+            pltpu.SemaphoreType.DMA((CAP, 2)),
+        ],
         compiler_params=pltpu.CompilerParams(vmem_limit_bytes=48 * 2**20),
         name="newton",
     )(tab, gathered)

time: 110 us -> 108 us (0.982); the launches traced: 110 us -> 107 us
  Pallas kernels: 109 us -> 105 us
    pallas_call x1, Pallas kernels: 102 us -> 99.1 us  [run_exchange(): pl.pallas_call(functools.partial(exchange, sure), out_shape=jax.ShapeDtyp...]
where the time goes in v2:
time: 108 us; the launch traced here: 107 us
  Pallas kernels  105 us (97%)
    pallas_call x1, Pallas kernels, run_exchange(): pl.pallas_call(functools.partial(exchange, sure), out_shape=jax.ShapeDtyp...  99.1 us
    pallas_call x1, Pallas kernels, per_device(): pl.pallas_call(functools.partial(newton, scale_out), out_shape=jax.ShapeD...  4.83 us

profile of v2, /device:TPU:33, one launch (start us, length us, event | category | flops | bytes accessed | tf_op | source)
XLA Modules:
  0.0 106.7 jit_solution(9771523908566110781)
XLA Ops:
  0.0 1.2 %tables.1.tab_ref = s32[16,128]{1,0:T(8,128)S(1)} custom-call(s32[1,256]{1,0:T(1,128)} %bitcast.23), custom_call_target="tpu_custom_call" | custom-call | tf_op jit(solution)/shard_map/tables/pallas_call | solution.py:447
  1.2 0.5 slice.4
  2.4 99.3 %conditional.1 = (bf16[2,2,2,32,2,16,128]{6,5,4,3,2,1,0:T(8,128)(2,1)S(1)}) conditional(s32[]{:T(128)} %bitcast.6, (s32[16,128]{1,0:T(8,128)S(1)}, bf16[256,32,256]{2,1,0:T(8,128)(2,1)}) %tuple.27, (s32[16,128]{1,0:T(8,128)S(1)}, bf16[256,32,256]{2,1,0:T(8,128)(2,1)}) %tuple.28, (s32[16,128]{1,0:T(8,128)S(1)}, ...), branch_computations={%region_0.0_spmd, %region_1.0_spmd, %region_2.0_spmd, %region_3.0_... | conditional | flops 136872000 | bytes 37762968 | solution.py:455
  2.4 99.1 %exchange25.1 = bf16[2,2,2,32,2,16,128]{6,5,4,3,2,1,0:T(8,128)(2,1)S(1)} custom-call(s32[16,128]{1,0:T(8,128)S(1)} %get-tuple-element.28.tab_ref, bf16[256,32,256]{2,1,0:T(8,128)(2,1)} %get-tuple-element.29.grads_ref), custom_call_target="tpu_custom_call" | custom-call | tf_op jit(solution)/shard_map/cond/branch_1_fun/exchange25/pallas_call | solution.py:300
  101.7 4.8 %newton.1 = bf16[2,2,32,2,16,256]{5,4,3,2,1,0:T(8,128)(2,1)} custom-call(s32[16,128]{1,0:T(8,128)S(1)} %tables.1.tab_ref, bf16[2,2,2,32,2,16,128]{6,5,4,3,2,1,0:T(8,128)(2,1)S(1)} %get-tuple-element.34.x_ref), custom_call_target="tpu_custom_call" | custom-call | tf_op jit(solution)/shard_map/newton/pallas_call | solution.py:456
